TPU v7x, 32 devices: a whole 2x2x4 slice. The times are simulated.
32 devices in a mesh: dp: 4 (over y, core), fsdp: 8 (over z, x).
Axes of the slice: x: 2, y: 2, z: 4, core: 2. Of those that a mesh axis runs over, the one named last changes fastest.
Arguments:
- activations: bfloat16 [4096, 8192], P(('dp', 'fsdp')), may hold values from -630 to 630, as said below
- gain: bfloat16 [8192], P('fsdp'), may hold values from 0.25 to 1.75
- key_weight: bfloat16 [8192, 512], P('fsdp'), may hold values from -0.0625 to 0.0625
- key_gain: float32 [128], replicated, may hold values from 0.25 to 1.75
- cotangent: bfloat16 [4096, 512], P(('dp', 'fsdp')), may hold values from -6 to 6
- directions: bfloat16 [8192, 8], P('fsdp'), may hold values from -6 to 6
Outputs:
- ortho_basis: float32 [8192, 8], P('fsdp')
- grad: float32 [8192], P('fsdp')
Inputs may be any that keep to these rules, and one draw needn't show every extreme that they name: The block's input activations.
All inputs are finite; a program needn't handle non-finite values.
Results may differ from a plain program's by a relative error of at most 0.01.
Values may be sent and summed in bfloat16 or wider, within the bound.
A program may use at most 128 MiB of HBM per device.

v0:
```python
import math

import jax
import jax.numpy as jnp
from jax import lax
from jax.sharding import PartitionSpec as P

D = 8192
HEADS_KV = 4
HEAD_DIM = 128


def key_stats(key_rows, weighted_flat):
    shaped = key_rows.reshape(key_rows.shape[0], HEADS_KV, HEAD_DIM)
    key_scale = jnp.sqrt(jnp.mean(shaped * shaped, axis=-1, keepdims=True) + 1e-05)
    unit_keys = shaped / key_scale
    weighted = weighted_flat.reshape(shaped.shape)
    inner_sum = jnp.sum(unit_keys * weighted, axis=-1, keepdims=True)
    grad_keys = (weighted - unit_keys * inner_sum / HEAD_DIM) / key_scale
    return (key_scale, unit_keys, weighted, inner_sum, grad_keys)


def second_order(tangent_keys, key_scale, unit_keys, weighted, inner_sum, grad_keys):
    shift_rate = jnp.sum(unit_keys * tangent_keys, axis=-1, keepdims=True) / HEAD_DIM
    unit_change = (tangent_keys - unit_keys * shift_rate) / key_scale
    along = jnp.sum(unit_change * weighted, axis=-1, keepdims=True)
    return (
        -(unit_change * inner_sum + unit_keys * along) / (HEAD_DIM * key_scale)
        - grad_keys * shift_rate / key_scale
    )


def project_rows(back_rows, normed, weight_rows):
    row_count = weight_rows.shape[0]
    block_width = math.gcd(row_count, 512)

    def project_one_block(position):
        offset = position * block_width
        weight_part = lax.dynamic_slice_in_dim(weight_rows, offset, block_width, 0)
        input_part = lax.dynamic_slice_in_dim(normed, offset, block_width, 1)
        product = jnp.dot(back_rows, weight_part.T, preferred_element_type=jnp.float32)
        product = product.reshape(-1, input_part.shape[0], block_width)
        return jnp.sum(product * input_part[None], axis=1)

    block_parts = lax.map(project_one_block, jnp.arange(row_count // block_width, dtype=jnp.int32))
    return jnp.transpose(block_parts, (1, 0, 2)).reshape(block_parts.shape[1], row_count)


def per_device(activations, gain, key_weight, key_gain, cotangent, directions):
    tokens_dev = activations.shape[0]
    total_tokens = tokens_dev * lax.axis_size("dp") * lax.axis_size("fsdp")
    values = activations.astype(jnp.float32)
    normed = values / jnp.sqrt(jnp.mean(values * values, axis=1, keepdims=True) + 1e-05)
    width_keys = key_weight.shape[1]
    count_dirs = directions.shape[1]
    initial = (
        jnp.zeros((tokens_dev, width_keys), jnp.float32),
        jnp.zeros((count_dirs * tokens_dev, width_keys), jnp.float32),
    )
    weight_rows = lax.all_gather(key_weight, "fsdp", axis=0, tiled=True)
    direction_rows = lax.all_gather(directions, "fsdp", axis=0, tiled=True)
    gain_rows = lax.all_gather(gain, "fsdp", axis=0, tiled=True)
    row_count = weight_rows.shape[0]
    block_width = math.gcd(row_count, 512)

    def forward_one_block(position, sums_now):
        key_sum, tangent_sum = sums_now
        offset = position * block_width
        weight_part = lax.dynamic_slice_in_dim(weight_rows, offset, block_width, 0)
        direction_part = lax.dynamic_slice_in_dim(direction_rows, offset, block_width, 0).astype(
            jnp.float32
        )
        gain_part = lax.dynamic_slice_in_dim(gain_rows, offset, block_width, 0).astype(jnp.float32)
        input_part = lax.dynamic_slice_in_dim(normed, offset, block_width, 1)
        scaled_in = (input_part * gain_part[None, :]).astype(jnp.bfloat16)
        key_sum = key_sum + jnp.dot(scaled_in, weight_part, preferred_element_type=jnp.float32)
        lifted = (input_part[None] * direction_part.T[:, None, :]).astype(jnp.bfloat16)
        tangent_sum = tangent_sum + jnp.dot(
            lifted.reshape(-1, block_width), weight_part, preferred_element_type=jnp.float32
        )
        return (key_sum, tangent_sum)

    key_rows, tangent_flat = lax.fori_loop(0, row_count // block_width, forward_one_block, initial)
    weighted_flat = cotangent.astype(jnp.float32) * jnp.tile(key_gain, HEADS_KV)[None, :]
    key_scale, unit_keys, weighted, inner_sum, grad_keys = key_stats(key_rows, weighted_flat)
    tangent_keys = tangent_flat.reshape(count_dirs, tokens_dev, HEADS_KV, HEAD_DIM)
    second = second_order(tangent_keys, key_scale, unit_keys, weighted, inner_sum, grad_keys)
    back_rows = jnp.concatenate([grad_keys[None], second], axis=0).astype(jnp.bfloat16)
    back_rows = back_rows.reshape(-1, width_keys)
    partial_terms = project_rows(
        back_rows, normed, lax.all_gather(key_weight, "fsdp", axis=0, tiled=True)
    )
    shared_rows = lax.psum_scatter(partial_terms, "fsdp", scatter_dimension=1, tiled=True)
    summed = lax.psum(shared_rows, "dp") / math.sqrt(total_tokens)
    images = summed[1:]
    gram_matrix = lax.psum(jnp.dot(images, images.T, precision=lax.Precision.HIGHEST), "fsdp")
    factor = jnp.linalg.cholesky(gram_matrix)
    ortho_basis = math.sqrt(D) * jax.scipy.linalg.solve_triangular(factor, images, lower=True)
    return (ortho_basis.T, summed[0])


def solution(mesh):
    placed = (
        P(("dp", "fsdp"), None),
        P("fsdp"),
        P("fsdp", None),
        P(),
        P(("dp", "fsdp"), None),
        P("fsdp", None),
    )
    return jax.shard_map(
        per_device,
        mesh=mesh,
        in_specs=placed,
        out_specs=(P("fsdp", None), P("fsdp")),
        check_vma=False,
    )
```

profile of v0, /device:TPU:0, one launch (start us, length us, event | category | flops | bytes accessed | tf_op | source)
XLA Modules:
  0.0 520.5 jit_solution(3332822978367095965)
XLA Ops:
  10.5 29.2 %all_gather.11 = bf16[8192]{0:T(1024)(128)(2,1)} all-gather(bf16[1024]{0:T(1024)(128)(2,1)S(1)} %copy-done.6), channel_id=1, replica_groups=mesh['dp'=4,'fsdp'=8] {'fsdp'}, dimensions={0}, use_global_device_ids=true | all-gather | bytes 18432 | tf_op jit(solution)/shard_map/all_gather | solution.py:62
  39.7 31.1 %all_gather.12 = bf16[8192,8]{0,1:T(8,128)(2,1)S(1)} all-gather(bf16[1024,8]{0,1:T(8,128)(2,1)S(1)} %copy-done.5), channel_id=1, replica_groups=mesh['dp'=4,'fsdp'=8] {'fsdp'}, dimensions={0}, use_global_device_ids=true | all-gather | bytes 147456 | tf_op jit(solution)/shard_map/all_gather | solution.py:61
  70.8 2.1 fusion.8
  72.9 2.5 convert_divide_fusion
  75.4 63.8 %all-gather.2.cloned.1.call-done = bf16[8192,512]{1,0:T(8,128)(2,1)} async-done(((bf16[1024,512]{1,0:T(8,128)(2,1)}), bf16[8192,512]{1,0:T(8,128)(2,1)}) %all-gather.2.cloned.1.call-update) | async-done | bytes 8388624 | tf_op jit(solution)/shard_map/all_gather | solution.py:91
  139.2 86.6 %while.27 = (s32[]{:T(128)}, f32[128,512]{1,0:T(8,128)S(1)}, f32[1024,512]{1,0:T(8,128)S(1)}, f32[128,8192]{1,0:T(8,128)}, bf16[8192]{0:T(1024)(128)(2,1)}, /*in...) while((s32[]{:T(128)}, f32[128,512]{1,0:T(8,128)S(1)}, ...), condition=%wide.region_2.0_spmd.clone, body=%wide.region_1.0_spmd.clone.sunk | while | flops 606343680 | bytes 8960693 | solution.py:83
  140.4 2.0 select_add_fusion.2
  145.8 2.0 select_add_fusion.2
  151.2 2.0 select_add_fusion.2
  156.6 2.0 select_add_fusion.2
  162.0 2.0 select_add_fusion.2
  164.8 1.4 convolution_add_fusion.2
  167.4 2.0 select_add_fusion.2
  170.2 1.4 convolution_add_fusion.2
  172.9 2.0 select_add_fusion.2
  175.6 1.4 convolution_add_fusion.2
  178.3 2.0 select_add_fusion.2
  183.7 2.0 select_add_fusion.2
  189.1 2.0 select_add_fusion.2
  194.5 2.0 select_add_fusion.2
  199.9 2.0 select_add_fusion.2
  205.4 2.0 select_add_fusion.2
  210.8 2.0 select_add_fusion.2
  216.2 2.0 select_add_fusion.2
  221.6 2.0 select_add_fusion.2
  226.3 1.7 reshape.127
  228.7 2.9 multiply_reduce_fusion.2
  232.1 45.4 %fusion.10 = bf16[8,128,4,128]{3,2,1,0:T(4,128)(2,1)S(1)} fusion(f32[128,4,128]{2,1,0:T(4,128)S(1)} %subtract_divide_fusion.1, f32[128,4]{1,0:T(8,128)S(1)} %get-tuple-element.220, f32[128,4,128]{2,1,0:T(4,128)S(1)} %copy-done.3, f32[128,4]{1,0:T(8,128)S(1)} %get-tuple-element.218, f32[128,4]{1,0:T(8,128)S(1)} %get-tuple-element.221, ...), kind=kOutput, calls=%fused_computation.27 | output fusion | flops 8392831 | bytes 3954688 | tf_op jit(solution)/shard_map/mul | solution.py:28
  278.5 137.3 %while.26 = (s32[]{:T(128)}, f32[16,9,512]{2,1,0:T(8,128)}, s32[16]{0:T(128)S(1)}, bf16[8192,512]{1,0:T(8,128)(2,1)}, bf16[1152,512]{1,0:T(8,128)(2,1)S(1)}, /*i...) while((s32[]{:T(128)}, f32[16,9,512]{2,1,0:T(8,128)}, s32[16]{0:T(128)S(1)}, ...), condition=%wide.region_9.10_spmd, body=%wide.region_7.9_spmd.sunk | while | flops 605154816 | bytes 11997863 | solution.py:45
  279.7 3.4 convolution_bitcast_fusion.2
  283.1 2.0 copy.28
  288.3 3.4 convolution_bitcast_fusion.2
  291.7 2.0 copy.28
  296.9 3.4 convolution_bitcast_fusion.2
  300.3 2.0 copy.28
  305.5 3.4 convolution_bitcast_fusion.2
  308.9 2.0 copy.28
  314.1 3.4 convolution_bitcast_fusion.2
  317.4 2.0 copy.28
  322.7 3.4 convolution_bitcast_fusion.2
  326.0 2.0 copy.28
  331.2 3.4 convolution_bitcast_fusion.2
  334.6 2.0 copy.28
  339.8 3.4 convolution_bitcast_fusion.2
  343.2 2.0 copy.28
  348.4 3.4 convolution_bitcast_fusion.2
  351.8 2.0 copy.28
  357.0 3.4 convolution_bitcast_fusion.2
  360.4 2.0 copy.28
  365.6 3.4 convolution_bitcast_fusion.2
  368.9 2.0 copy.28
  374.2 3.4 convolution_bitcast_fusion.2
  377.5 2.0 copy.28
  382.7 3.4 convolution_bitcast_fusion.2
  386.1 2.0 copy.28
  391.3 3.4 convolution_bitcast_fusion.2
  394.7 2.0 copy.28
  399.9 3.4 convolution_bitcast_fusion.2
  403.3 2.0 copy.28
  408.5 3.4 convolution_bitcast_fusion.2
  411.9 2.0 copy.28
  418.2 60.4 %reduce-scatter.2.cloned.1.call-done = f32[9,1024]{1,0:T(8,128)} async-done(((f32[9,8192]{1,0:T(8,128)}), f32[9,1024]{1,0:T(8,128)}) %reduce-scatter.2.cloned.1.call-update) | async-done | bytes 36880 | tf_op jit(solution)/shard_map/reduce_scatter | solution.py:93
  478.6 11.2 %psum.14 = f32[9,1024]{1,0:T(8,128)S(1)} all-reduce(f32[9,1024]{1,0:T(8,128)} %reduce-scatter.2.cloned.1.call-done), channel_id=1, replica_groups=mesh['dp'=4,'fsdp'=8] {'dp'}, use_global_device_ids=true, to_apply=%region_11.12 | all-reduce | flops 9216 | bytes 73728 | tf_op jit(solution)/shard_map/psum | solution.py:94
  490.6 19.4 %psum.15 = f32[8,8]{0,1:T(8,128)S(1)} all-reduce(f32[8,8]{0,1:T(8,128)S(1)} %fusion.16), channel_id=1, replica_groups=mesh['dp'=4,'fsdp'=8] {'fsdp'}, use_global_device_ids=true, to_apply=%region_12.13 | all-reduce | flops 64 | bytes 512 | tf_op jit(solution)/shard_map/psum | solution.py:96
  (192 shorter events, 102.2 us)
Async XLA Ops:
  7.2 0.8 copy-start
  7.2 3.4 copy-start.6
  7.2 32.6 %copy-start.5 = (bf16[1024,8]{0,1:T(8,128)(2,1)S(1)}, bf16[1024,8]{0,1:T(8,128)(2,1)}, u32[]{:S(2)}) copy-start(bf16[1024,8]{0,1:T(8,128)(2,1)} %param.15) | copy-start | bytes 49156
  7.2 132.0 %all-gather.2.cloned.1.call-start = ((), (), s32[]{:S(2)}) async-start(), calls=%async_computation.1 | async-start | bytes 9437184 | tf_op jit(solution)/shard_map/all_gather | solution.py:91
  7.9 470.7 %reduce-scatter.2.cloned.1.call-start = ((), (), s32[]{:S(2)}) async-start(), calls=%async_computation.2 | async-start | bytes 589824 | tf_op jit(solution)/shard_map/reduce_scatter | solution.py:93
  10.5 62.4 %copy-start.1 = (bf16[128,8192]{1,0:T(8,128)(2,1)S(1)}, bf16[128,8192]{1,0:T(8,128)(2,1)}, u32[]{:S(2)}) copy-start(bf16[128,8192]{1,0:T(8,128)(2,1)} %param.10) | copy-start | bytes 6291460
  226.2 1.8 copy-start.3
  228.7 3.0 copy-start.4
  228.7 3.4 copy-start.2
Sparse Core Ops, SparseCore 0:
  10.2 128.9 all-gather.1
  418.4 60.1 reduce-scatter.1
where the time goes:
time: 525 us; the launch traced here: 520 us
  waiting for transfers between devices  125 us (24%)
  matrix products  109 us (21%)
  blocking collectives  90.9 us (17%)
  local copies, waits for them, and re-layouts  89.6 us (17%)
  other arithmetic  80.1 us (15%)
  between operations  14.3 us (3%)
  loops' own time  11.7 us (2%)
    all_gather x1, waiting for transfers between devices, per_device(): lax.all_gather(key_weight, 'fsdp', axis=0, tiled=True)  63.8 us
    reduce_scatter x1, waiting for transfers between devices, per_device(): lax.psum_scatter(partial_terms, 'fsdp', scatter_dimension=1, tiled=True)  60.4 us
    dot_general x16, matrix products, project_one_block(): jnp.dot(back_rows, weight_part.T, preferred_element_type=jnp.float32)  53.8 us
    mul x1, other arithmetic, second_order(): unit_keys * along  45.4 us
    dot_general x16, local copies, waits for them, and re-layouts, project_one_block(): jnp.dot(back_rows, weight_part.T, preferred_element_type=jnp.float32)  32.5 us
    dot_general x16, matrix products, forward_one_block(): jnp.dot(lifted.reshape(-1, block_width), weight_part, preferred_element_t...  32.1 us
    all_gather x1, blocking collectives, per_device(): direction_rows = lax.all_gather(directions, 'fsdp', axis=0, tiled=True)  31.1 us
    all_gather x1, blocking collectives, per_device(): gain_rows = lax.all_gather(gain, 'fsdp', axis=0, tiled=True)  29.2 us
  transfers between devices with their start and end apart: 2, of which 2 were waited for; matrix products, arithmetic and copies ran while one was open for 1% of the time, Pallas kernels for 0%

commit v1 on v0

v1 whole, which is shorter than its diff:
```python
import functools
import math

import jax
import jax.numpy as jnp
from jax import lax
from jax.experimental import pallas as pl
from jax.experimental.pallas import tpu as pltpu
from jax.sharding import PartitionSpec as P

D = 8192
HEADS_KV = 4
HEAD_DIM = 128
PAD = 16
MESH = pl.DeviceIdType.MESH
Z, Y1, DZ, DY1, X, Y2, DX, DY2 = range(8)
ZB = 8
F32 = jnp.float32


def kernel(
    n, n_dp, groups, total_tokens,
    act_ref, w_ref, dg_ref, key_gain_ref, cot_ref,
    ortho_ref, grad_ref,
    wbuf, lifted, acc, back, part, rbuf, xbuf, gbuf, rstd,
    send_sem, recv_sem, part_send, part_recv, dp_send, dp_recv, gram_send, gram_recv,
):
    line = n // 2
    steps = line * groups
    tokens = act_ref.shape[0]
    rows = w_ref.shape[0]
    rows_g = rows // (2 * groups)
    unit = rows_g // 4
    count = back.shape[0] // tokens
    dp, me = lax.axis_index("dp"), lax.axis_index("fsdp")
    core, y = lax.rem(dp, 2), dp // 2
    z, x = me // 2, lax.rem(me, 2)
    sibling = dp + 1 - 2 * core
    y_peer = lax.rem(dp + 2, n_dp)
    x_peer = me + 1 - 2 * x

    barrier = pltpu.get_barrier_semaphore()

    def greet_fsdp(b, _):
        pl.semaphore_signal(
            barrier, inc=1, device_id=(dp, lax.rem(me + 1 + b, n)), device_id_type=MESH
        )
        return 0

    def greet_dp(b, _):
        pl.semaphore_signal(
            barrier, inc=1, device_id=(lax.rem(dp + 1 + b, n_dp), me), device_id_type=MESH
        )
        return 0

    lax.fori_loop(0, n - 1, greet_fsdp, 0)
    lax.fori_loop(0, n_dp - 1, greet_dp, 0)

    def place(zp, xp, cp, g):
        return ((zp * 2 + xp) * 2 + cp) * groups + g

    for cg in range(2 * groups):
        at = me * 2 * groups + cg
        wbuf[at, 0 : 2 * unit] = w_ref[cg * rows_g : cg * rows_g + 2 * unit]
        wbuf[at, 2 * unit : 2 * unit + PAD] = dg_ref[cg]
        wbuf[at, 2 * unit + PAD :] = w_ref[cg * rows_g + 2 * unit : (cg + 1) * rows_g]

    room = jnp.minimum(z, line - 1 - z)
    wide = jnp.where(z < line - 1 - z, 1, -1)

    def source(k):
        near = k <= 2 * room
        dist = jnp.where(near, (k + 1) // 2, k - room)
        sign = jnp.where(near, jnp.where(lax.rem(k, 2) == 1, -1, 1), wide)
        return z + sign * dist, sign

    def span(kind, first, sent):
        side = y if sent else 1 - y
        if kind in (Z, ZB, DZ) or (first and kind in (X, DX)):
            start, size = y * unit, 3 * unit + PAD
        elif kind in (X, DX):
            start, size = y * (2 * unit), 2 * unit + PAD
        else:
            if kind in (DY1, DY2):
                side = 1 - y if sent else y
                side = 1 - y
            if kind in (Y1, DY1) or first:
                start, size = side * (3 * unit + PAD), unit
            else:
                start, size = side * (2 * unit + PAD), 2 * unit
        return pl.ds(pl.multiple_of(start, 16), size)

    def copy(kind, i, first, sent):
        k, g = i // groups, lax.rem(i, groups)
        zp, sign = source(k)
        own_column = kind in (Z, ZB, Y1, DZ, DY1)
        to_sibling = kind in (DZ, DY1, DX, DY2)
        if kind == X and sent:
            own_column = True
        column = x if own_column else 1 - x
        half = (core if sent else 1 - core) if to_sibling else core
        if kind == ZB:
            device = (dp, me - 2)
        elif kind == Z:
            device = (dp, me + 2) if first else (dp, me - 2 * sign)
        elif kind == X:
            device = (dp, x_peer)
        elif kind in (Y1, Y2):
            device = (y_peer, me)
        else:
            device = (sibling, me)
        ref = wbuf.at[place(zp, column, half, g), span(kind, first, sent)]
        arrival = Z if kind == ZB else kind
        return pltpu.make_async_remote_copy(
            src_ref=ref,
            dst_ref=ref,
            send_sem=send_sem.at[kind, i],
            recv_sem=recv_sem.at[arrival, zp * groups + g],
            device_id=device,
            device_id_type=MESH,
        )

    def start(kind, i, first=False):
        copy(kind, i, first, True).start()

    def arrive(kind, i, first=False):
        copy(kind, i, first, False).wait_recv()

    def sent(kind, i, first=False):
        copy(kind, i, first, True).wait_send()

    def passes_on(i):
        sign = source(i // groups)[1]
        onward = z - sign
        return (onward >= 0) & (onward < line)

    def square_sum(q, run):
        part_in = act_ref[:, pl.ds(pl.multiple_of(q * 512, 512), 512)].astype(F32)
        return run + jnp.sum(part_in * part_in, axis=1, keepdims=True)

    width = act_ref.shape[1]
    square = lax.fori_loop(0, width // 512, square_sum, jnp.zeros((tokens, 1), F32))
    rstd[...] = jnp.broadcast_to(1.0 / jnp.sqrt(square / width + 1e-05), rstd.shape)
    acc[...] = jnp.zeros_like(acc)

    pl.semaphore_wait(barrier, n - 1 + n_dp - 1)

    for g in range(groups):

        @pl.when(z + 1 < line)
        def _():
            start(Z, g, True)

        @pl.when(z >= 1)
        def _():
            start(ZB, g, True)

        start(X, g, True)

    def normed_at(feature, size):
        values = act_ref[:, pl.ds(pl.multiple_of(feature, 128), size)].astype(F32)
        return values * rstd[:, 0:1]

    def weight_at(at):
        return jnp.concatenate(
            [wbuf[at, 0 : 2 * unit], wbuf[at, 2 * unit + PAD : 4 * unit + PAD]], axis=0
        )

    def forward(zp, xp, g):
        for cp in range(2):
            at = place(zp, xp, cp, g)
            normed = normed_at((zp * 2 + xp) * rows + (cp * groups + g) * rows_g, rows_g)
            factors = wbuf[at, 2 * unit : 2 * unit + PAD, 0:rows_g].astype(F32)
            for j in range(count):
                lifted[j * tokens : (j + 1) * tokens, cp * rows_g : (cp + 1) * rows_g] = (
                    normed * factors[j : j + 1]
                ).astype(jnp.bfloat16)
        weight = jnp.concatenate(
            [weight_at(place(zp, xp, 0, g)), weight_at(place(zp, xp, 1, g))], axis=0
        )
        for h in range(2):
            half = slice(h * 256, (h + 1) * 256)
            acc[:, half] += jnp.dot(
                lifted[...], weight[:, half], preferred_element_type=F32
            )

    def forward_own(g, _):
        forward(z, x, g)
        return 0

    lax.fori_loop(0, groups, forward_own, 0)

    def cross_arrived(i, first):
        arrive(X, i, first)
        start(Y2, i, first)
        start(DX, i, first)

    def turn(t, _):
        i = t + groups

        @pl.when(i < steps)
        def _():
            arrive(Z, i)

            @pl.when(passes_on(i))
            def _():
                start(Z, i)

            start(X, i)
            start(Y1, i)
            start(DZ, i)

        if groups > 1:

            @pl.when(t == 0)
            def _():
                for early in range(groups - 1):
                    cross_arrived(early, True)

        i1 = t + groups - 1

        @pl.when(i1 < groups)
        def _():
            cross_arrived(i1, True)

        @pl.when((i1 >= groups) & (i1 < steps))
        def _():
            cross_arrived(i1, False)
            arrive(Y1, i1)
            start(DY1, i1)

        i2 = t + groups - 2

        @pl.when((i2 >= 0) & (i2 < groups))
        def _():
            arrive(Y2, i2, True)
            start(DY2, i2, True)

        @pl.when((i2 >= groups) & (i2 < steps))
        def _():
            arrive(Y2, i2)
            start(DY2, i2)
            arrive(DZ, i2)
            arrive(DY1, i2)
            forward(source(i2 // groups)[0], x, lax.rem(i2, groups))

        i3 = t + groups - 3

        @pl.when((i3 >= 0) & (i3 < groups))
        def _():
            arrive(DX, i3, True)
            arrive(DY2, i3, True)

        @pl.when((i3 >= groups) & (i3 < steps))
        def _():
            arrive(DX, i3)
            arrive(DY2, i3)

        @pl.when((i3 >= 0) & (i3 < steps))
        def _():
            forward(source(i3 // groups)[0], 1 - x, lax.rem(i3, groups))

        return 0

    lax.fori_loop(0, steps + 3 - groups, turn, 0)

    for h in range(HEADS_KV):
        cols = slice(h * HEAD_DIM, (h + 1) * HEAD_DIM)
        key = acc[0:tokens, cols]
        inv_scale = 1.0 / jnp.sqrt(
            jnp.sum(key * key, axis=1, keepdims=True) / HEAD_DIM + 1e-05
        )
        unit_key = key * inv_scale
        weighted = cot_ref[:, cols].astype(F32) * key_gain_ref[...]
        inner = jnp.sum(unit_key * weighted, axis=1, keepdims=True)
        back[0:tokens, cols] = (
            (weighted - unit_key * (inner / HEAD_DIM)) * inv_scale
        ).astype(jnp.bfloat16)
        inv_square = inv_scale * inv_scale

        def one_direction(j, _):
            at = pl.ds(pl.multiple_of(j * tokens, 128), tokens)
            tangent = acc[at, cols]
            shift = jnp.sum(unit_key * tangent, axis=1, keepdims=True) / HEAD_DIM
            across = jnp.sum(weighted * tangent, axis=1, keepdims=True)
            by_tangent = -inner * inv_square / HEAD_DIM
            by_key = (3.0 * shift * inner - across) * inv_square / HEAD_DIM
            by_weight = -shift * inv_square
            back[at, cols] = (
                tangent * by_tangent + unit_key * by_key + weighted * by_weight
            ).astype(jnp.bfloat16)
            return 0

        lax.fori_loop(1, count, one_direction, 0)

    def terms_of(owner):
        def one_group(cg, _):
            weight = weight_at(owner * 2 * groups + cg)
            normed = normed_at(owner * rows + cg * rows_g, rows_g)
            product = lax.dot_general(
                back[...], weight, (((1,), (1,)), ((), ())), preferred_element_type=F32
            )
            cols = pl.ds(pl.multiple_of(cg * rows_g, 128), rows_g)
            for j in range(count):
                part[owner, j : j + 1, cols] = jnp.sum(
                    product[j * tokens : (j + 1) * tokens] * normed, axis=0, keepdims=True
                )
            return 0

        lax.fori_loop(0, 2 * groups, one_group, 0)

    def part_copy(b):
        owner = lax.rem(me + 1 + b, n)
        return pltpu.make_async_remote_copy(
            src_ref=part.at[owner],
            dst_ref=rbuf.at[me],
            send_sem=part_send.at[owner],
            recv_sem=part_recv.at[me],
            device_id=(dp, owner),
            device_id_type=MESH,
        )

    def send_part(b, _):
        terms_of(lax.rem(me + 1 + b, n))
        part_copy(b).start()
        return 0

    lax.fori_loop(0, n - 1, send_part, 0)
    terms_of(me)

    def take_part(b, run):
        other = lax.rem(me + n - 1 - b, n)
        pltpu.make_async_remote_copy(
            src_ref=part.at[other],
            dst_ref=rbuf.at[other],
            send_sem=part_send.at[other],
            recv_sem=part_recv.at[other],
            device_id=(dp, other),
            device_id_type=MESH,
        ).wait_recv()
        return run + rbuf[other]

    xbuf[dp] = lax.fori_loop(0, n - 1, take_part, part[me])

    def dp_copy(b, slot):
        other = lax.rem(dp + 1 + b, n_dp)
        return pltpu.make_async_remote_copy(
            src_ref=xbuf.at[dp if slot else other],
            dst_ref=xbuf.at[dp if slot else other],
            send_sem=dp_send.at[b],
            recv_sem=dp_recv.at[dp if slot else other],
            device_id=(other, me),
            device_id_type=MESH,
        )

    for b in range(n_dp - 1):
        dp_copy(b, True).start()
    for b in range(n_dp - 1):
        dp_copy(b, False).wait_recv()
    summed = xbuf[0]
    for d in range(1, n_dp):
        summed = summed + xbuf[d]
    summed = summed / math.sqrt(total_tokens)
    grad_ref[...] = summed[0:1]
    images = summed[1:count]
    dirs = count - 1
    lane = lax.broadcasted_iota(jnp.int32, (dirs, 128), 1)
    gram = jnp.zeros((dirs, 128), F32)
    for j in range(dirs):
        gram = jnp.where(
            lane == j, jnp.sum(images * images[j : j + 1], axis=1, keepdims=True), gram
        )
    gbuf[me] = gram

    def gram_copy(b, slot):
        other = lax.rem(me + 1 + b, n)
        return pltpu.make_async_remote_copy(
            src_ref=gbuf.at[me if slot else other],
            dst_ref=gbuf.at[me if slot else other],
            send_sem=gram_send.at[b],
            recv_sem=gram_recv.at[me if slot else other],
            device_id=(dp, other),
            device_id_type=MESH,
        )

    def start_gram(b, _):
        gram_copy(b, True).start()
        return 0

    def take_gram(b, _):
        gram_copy(b, False).wait_recv()
        return 0

    lax.fori_loop(0, n - 1, start_gram, 0)
    lax.fori_loop(0, n - 1, take_gram, 0)
    gram = lax.fori_loop(1, n, lambda s, run: run + gbuf[s], gbuf[0])

    row = lax.broadcasted_iota(jnp.int32, (dirs, 1), 0)
    for j in range(dirs):
        inverse = 1.0 / jnp.sqrt(gram[j : j + 1, j : j + 1])
        gram_row = gram[j : j + 1] * inverse
        image_row = images[j : j + 1] * inverse
        factor = jnp.where(row > j, gram[:, j : j + 1] * inverse, 0.0)
        gram = jnp.where(row == j, gram_row, gram - factor * gram_row)
        images = jnp.where(row == j, image_row, images - factor * image_row)
    ortho_ref[...] = math.sqrt(D) * images

    for g in range(groups):

        @pl.when(z + 1 < line)
        def _():
            sent(Z, g, True)

        @pl.when(z >= 1)
        def _():
            sent(ZB, g, True)

        for kind in (X, Y2, DX, DY2):
            sent(kind, g, True)

    def drain(i, _):
        @pl.when(passes_on(i))
        def _():
            sent(Z, i)

        for kind in (X, Y1, DZ, DY1, Y2, DX, DY2):
            sent(kind, i)
        return 0

    lax.fori_loop(groups, steps, drain, 0)

    def drain_parts(b, _):
        part_copy(b).wait_send()
        gram_copy(b, True).wait_send()
        return 0

    lax.fori_loop(0, n - 1, drain_parts, 0)
    for b in range(n_dp - 1):
        dp_copy(b, True).wait_send()


def per_device(n, n_dp, activations, gain, key_weight, key_gain, cotangent, directions):
    tokens, width = activations.shape
    rows, width_keys = key_weight.shape
    count = directions.shape[1] + 1
    groups = 2 if rows >= 1024 else 1
    rows_g = rows // (2 * groups)
    steps = n // 2 * groups
    factors = jnp.concatenate(
        [gain[None], directions.T, jnp.zeros((PAD - count, rows), jnp.bfloat16)], axis=0
    )
    factors = factors.reshape(PAD, 2 * groups, rows_g).transpose(1, 0, 2)
    factors = jnp.pad(factors, ((0, 0), (0, 0), (0, width_keys - rows_g)))
    vmem = pl.BlockSpec(memory_space=pltpu.VMEM)
    dma = pltpu.SemaphoreType.DMA
    flops = 4 * count * tokens * width * width_keys
    ortho, grad = pl.pallas_call(
        functools.partial(kernel, n, n_dp, groups, tokens * n * n_dp),
        out_shape=(
            jax.ShapeDtypeStruct((count - 1, rows), F32),
            jax.ShapeDtypeStruct((1, rows), F32),
        ),
        in_specs=[vmem] * 5,
        out_specs=(vmem, vmem),
        scratch_shapes=[
            pltpu.VMEM((n * 2 * groups, rows_g + PAD, width_keys), jnp.bfloat16),
            pltpu.VMEM((count * tokens, 2 * rows_g), jnp.bfloat16),
            pltpu.VMEM((count * tokens, width_keys), F32),
            pltpu.VMEM((count * tokens, width_keys), jnp.bfloat16),
            pltpu.VMEM((n, count, rows), F32),
            pltpu.VMEM((n, count, rows), F32),
            pltpu.VMEM((n_dp, count, rows), F32),
            pltpu.VMEM((n, count - 1, 128), F32),
            pltpu.VMEM((tokens, 128), F32),
            dma((9, steps)),
            dma((8, steps)),
            dma((n,)),
            dma((n,)),
            dma((n_dp,)),
            dma((n_dp,)),
            dma((n,)),
            dma((n,)),
        ],
        compiler_params=pltpu.CompilerParams(
            collective_id=0, has_side_effects=True, vmem_limit_bytes=48 * 1024 * 1024
        ),
        cost_estimate=pl.CostEstimate(flops=flops, bytes_accessed=4 * 2**20, transcendentals=0),
    )(activations, key_weight, factors, key_gain[None], cotangent)
    return (ortho.T, grad[0])


def solution(mesh):
    placed = (
        P(("dp", "fsdp"), None),
        P("fsdp"),
        P("fsdp", None),
        P(),
        P(("dp", "fsdp"), None),
        P("fsdp", None),
    )
    return jax.shard_map(
        functools.partial(per_device, mesh.shape["fsdp"], mesh.shape["dp"]),
        mesh=mesh,
        in_specs=placed,
        out_specs=(P("fsdp", None), P("fsdp")),
        check_vma=False,
    )
```

time: 525 us -> 95.2 us (0.18)
  waiting for transfers between devices: 125 us -> 0 us
  matrix products: 109 us -> 0 us
  blocking collectives: 90.9 us -> 0 us
  Pallas kernels: 0 us -> 87.1 us
  local copies, waits for them, and re-layouts: 89.6 us -> 6.36 us
  other arithmetic: 80.1 us -> 0.79 us
  between operations: 14.3 us -> 0.66 us
  loops' own time: 11.7 us -> 0 us
    dot_general x49 -> x0, matrix products: 108 us -> none  [the longest x16 53.8 us: project_one_block(): jnp.dot(back_rows, weight_part.T, preferred_element_type=jnp.float32)]
    pallas_call x0 -> x1, Pallas kernels: none -> 87.1 us  [per_device(): pl.pallas_call(functools.partial(kernel, n, n_dp, groups, tokens * n * n_...]
    all_gather x1 -> x0, waiting for transfers between devices: 63.8 us -> none  [per_device(): lax.all_gather(key_weight, 'fsdp', axis=0, tiled=True)]
    reduce_scatter x1 -> x0, waiting for transfers between devices: 60.4 us -> none  [per_device(): lax.psum_scatter(partial_terms, 'fsdp', scatter_dimension=1, tiled=True)]
    all_gather x2 -> x0, blocking collectives: 60.3 us -> none  [the longest x1 31.1 us: per_device(): direction_rows = lax.all_gather(directions, 'fsdp', axis=0, tiled=True)]
    mul x3 -> x0, other arithmetic: 46.4 us -> none  [the longest x1 45.4 us: second_order(): unit_keys * along]
    dynamic_slice x48 -> x0, local copies, waits for them, and re-layouts: 40.5 us -> none  [the longest x16 15.6 us: project_one_block(): input_part = lax.dynamic_slice_in_dim(normed, offset, block_width, 1)]
    dot_general x16 -> x0, local copies, waits for them, and re-layouts: 32.5 us -> none  [project_one_block(): jnp.dot(back_rows, weight_part.T, preferred_element_type=jnp.float32)]
  transfers between devices with their start and end apart: 2 -> 0, of which waited for: 2 -> 0; matrix products, arithmetic and copies ran while one was open for 1% -> 0% of each run, Pallas kernels for 0% -> 0%
where the time goes in v1:
time: 95.2 us; the launch traced here: 94.9 us
  Pallas kernels  87.1 us (91%)
  local copies, waits for them, and re-layouts  6.36 us (7%)
    pallas_call x1, Pallas kernels, per_device(): pl.pallas_call(functools.partial(kernel, n, n_dp, groups, tokens * n * n_...  87.1 us
    unnamed x10, local copies, waits for them, and re-layouts  5.58 us

profile of v1, /device:TPU:0, one launch (start us, length us, event | category | flops | bytes accessed | tf_op | source)
XLA Modules:
  0.0 94.9 jit_solution(4228059511781481229)
XLA Ops:
  0.6 0.1 pad.7.clone
  0.7 0.7 concatenate.11
  1.4 0.8 maximum_bitcast_fusion
  2.2 0.0 copy-start
  2.2 1.6 %copy-done = bf16[128,8192]{1,0:T(8,128)(2,1)S(1)} copy-done((bf16[128,8192]{1,0:T(8,128)(2,1)S(1)}, bf16[128,8192]{1,0:T(8,128)(2,1)}, u32[]{:S(2)}) %copy-start) | copy-done | bytes 2097176
  3.8 0.0 copy-start.1
  3.8 1.2 %copy-done.1 = bf16[1024,512]{1,0:T(8,128)(2,1)S(1)} copy-done((bf16[1024,512]{1,0:T(8,128)(2,1)S(1)}, bf16[1024,512]{1,0:T(8,128)(2,1)}, u32[]{:S(2)}) %copy-start.1) | copy-done | bytes 1048600
  5.0 0.0 copy-start.2
  5.0 0.9 copy-done.2
  5.9 0.0 copy-start.3
  5.9 0.7 copy-done.3
  6.6 87.1 %shard_map.77 = (f32[8,1024]{1,0:T(8,128)S(1)}, f32[1,1024]{1,0:T(1,128)S(1)}) custom-call(bf16[128,8192]{1,0:T(8,128)(2,1)S(1)} %copy-done, bf16[1024,512]{1,0:T(8,128)(2,1)S(1)} %copy-done.1, bf16[4,16,512]{2,1,0:T(8,128)(2,1)S(1)} %pad.4.dg_ref, f32[1,128]{1,0:T(1,128)S(1)} %bitcast.10, bf16[128,512]{1,0:T(8,128)(2,1)S(1)} %copy-done.2), custom_call_target="tpu_custom_call" | custom-call | flops 19327352832 | bytes 4194304 | tf_op jit(solution)/shard_map/pallas_call | solution.py:457
  93.7 0.6 copy.11
  94.3 0.6 copy.12
  (2 shorter events, 0.0 us)
Async XLA Ops:
  2.2 1.6 %copy-start = (bf16[128,8192]{1,0:T(8,128)(2,1)S(1)}, bf16[128,8192]{1,0:T(8,128)(2,1)}, u32[]{:S(2)}) copy-start(bf16[128,8192]{1,0:T(8,128)(2,1)} %act_ref.1) | copy-start | bytes 6291460
  3.8 1.2 %copy-start.1 = (bf16[1024,512]{1,0:T(8,128)(2,1)S(1)}, bf16[1024,512]{1,0:T(8,128)(2,1)}, u32[]{:S(2)}) copy-start(bf16[1024,512]{1,0:T(8,128)(2,1)} %w_ref.1) | copy-start | bytes 3145732
  5.0 0.9 copy-start.2
  5.9 0.7 copy-start.3

commit v2 on v1

--- a/solution.py
+++ b/solution.py
@@ -20,9 +20,9 @@
 
 def kernel(
     n, n_dp, groups, total_tokens,
-    act_ref, w_ref, dg_ref, key_gain_ref, cot_ref,
+    act_in, w_ref, dg_ref, key_gain_ref, cot_in,
     ortho_ref, grad_ref,
-    wbuf, lifted, acc, back, part, rbuf, xbuf, gbuf, rstd,
+    act_ref, cot_ref, wbuf, lifted, acc, back, part, rbuf, xbuf, gbuf, nbuf, own_sem, in_sem,
     send_sem, recv_sem, part_send, part_recv, dp_send, dp_recv, gram_send, gram_recv,
 ):
     line = n // 2
@@ -59,11 +59,29 @@
     def place(zp, xp, cp, g):
         return ((zp * 2 + xp) * 2 + cp) * groups + g
 
+    own_copies = []
     for cg in range(2 * groups):
         at = me * 2 * groups + cg
-        wbuf[at, 0 : 2 * unit] = w_ref[cg * rows_g : cg * rows_g + 2 * unit]
-        wbuf[at, 2 * unit : 2 * unit + PAD] = dg_ref[cg]
-        wbuf[at, 2 * unit + PAD :] = w_ref[cg * rows_g + 2 * unit : (cg + 1) * rows_g]
+        top, low = cg * rows_g, cg * rows_g + 2 * unit
+        own_copies += [
+            pltpu.make_async_copy(
+                w_ref.at[top : top + 2 * unit], wbuf.at[at, 0 : 2 * unit], own_sem.at[0, cg]
+            ),
+            pltpu.make_async_copy(
+                w_ref.at[low : low + 2 * unit],
+                wbuf.at[at, 2 * unit + PAD : 4 * unit + PAD],
+                own_sem.at[1, cg],
+            ),
+            pltpu.make_async_copy(
+                dg_ref.at[cg], wbuf.at[at, 2 * unit : 2 * unit + PAD], own_sem.at[2, cg]
+            ),
+        ]
+    for one in own_copies:
+        one.start()
+    act_copy = pltpu.make_async_copy(act_in, act_ref, in_sem.at[0])
+    cot_copy = pltpu.make_async_copy(cot_in, cot_ref, in_sem.at[1])
+    act_copy.start()
+    cot_copy.start()
 
     room = jnp.minimum(z, line - 1 - z)
     wide = jnp.where(z < line - 1 - z, 1, -1)
@@ -134,32 +152,47 @@
         onward = z - sign
         return (onward >= 0) & (onward < line)
 
+    pl.semaphore_wait(barrier, n - 1 + n_dp - 1)
+    for one in own_copies:
+        one.wait()
+
+    for g in range(groups):
+
+        @pl.when(z + 1 < line)
+        def _():
+            start(Z, g, True)
+
+        @pl.when(z >= 1)
+        def _():
+            start(ZB, g, True)
+
+        start(X, g, True)
+
+    acc[...] = jnp.zeros_like(acc)
+    act_copy.wait()
+
+    width = act_ref.shape[1]
+
     def square_sum(q, run):
         part_in = act_ref[:, pl.ds(pl.multiple_of(q * 512, 512), 512)].astype(F32)
-        return run + jnp.sum(part_in * part_in, axis=1, keepdims=True)
-
-    width = act_ref.shape[1]
-    square = lax.fori_loop(0, width // 512, square_sum, jnp.zeros((tokens, 1), F32))
-    rstd[...] = jnp.broadcast_to(1.0 / jnp.sqrt(square / width + 1e-05), rstd.shape)
-    acc[...] = jnp.zeros_like(acc)
-
-    pl.semaphore_wait(barrier, n - 1 + n_dp - 1)
-
-    for g in range(groups):
-
-        @pl.when(z + 1 < line)
-        def _():
-            start(Z, g, True)
-
-        @pl.when(z >= 1)
-        def _():
-            start(ZB, g, True)
-
-        start(X, g, True)
+        part_in = part_in * part_in
+        for h in range(4):
+            run = run + part_in[:, h * 128 : (h + 1) * 128]
+        return run
+
+    square = lax.fori_loop(0, width // 512, square_sum, jnp.zeros((tokens, 128), F32))
+    square = jnp.sum(square, axis=1, keepdims=True)
+    rstd = jnp.broadcast_to(1.0 / jnp.sqrt(square / width + 1e-05), (tokens, 512))
+
+    def normalize(q, _):
+        cols = pl.ds(pl.multiple_of(q * 512, 512), 512)
+        nbuf[:, cols] = act_ref[:, cols].astype(F32) * rstd
+        return 0
+
+    lax.fori_loop(0, width // 512, normalize, 0)
 
     def normed_at(feature, size):
-        values = act_ref[:, pl.ds(pl.multiple_of(feature, 128), size)].astype(F32)
-        return values * rstd[:, 0:1]
+        return nbuf[:, pl.ds(pl.multiple_of(feature, 128), size)]
 
     def weight_at(at):
         return jnp.concatenate(
@@ -264,6 +297,7 @@
 
     lax.fori_loop(0, steps + 3 - groups, turn, 0)
 
+    cot_copy.wait()
     for h in range(HEADS_KV):
         cols = slice(h * HEAD_DIM, (h + 1) * HEAD_DIM)
         key = acc[0:tokens, cols]
@@ -291,23 +325,24 @@
             ).astype(jnp.bfloat16)
             return 0
 
-        lax.fori_loop(1, count, one_direction, 0)
+        lax.fori_loop(1, count, one_direction, 0, unroll=True)
 
     def terms_of(owner):
-        def one_group(cg, _):
-            weight = weight_at(owner * 2 * groups + cg)
-            normed = normed_at(owner * rows + cg * rows_g, rows_g)
+        def one_pair(pair, _):
+            cg = owner * 2 * groups + 2 * pair
+            weight = jnp.concatenate([weight_at(cg), weight_at(cg + 1)], axis=0)
+            normed = normed_at(owner * rows + pair * 2 * rows_g, 2 * rows_g)
             product = lax.dot_general(
                 back[...], weight, (((1,), (1,)), ((), ())), preferred_element_type=F32
             )
-            cols = pl.ds(pl.multiple_of(cg * rows_g, 128), rows_g)
+            cols = pl.ds(pl.multiple_of(pair * 2 * rows_g, 128), 2 * rows_g)
             for j in range(count):
                 part[owner, j : j + 1, cols] = jnp.sum(
                     product[j * tokens : (j + 1) * tokens] * normed, axis=0, keepdims=True
                 )
             return 0
 
-        lax.fori_loop(0, 2 * groups, one_group, 0)
+        lax.fori_loop(0, groups, one_pair, 0)
 
     def part_copy(b):
         owner = lax.rem(me + 1 + b, n)
@@ -452,6 +487,7 @@
     factors = factors.reshape(PAD, 2 * groups, rows_g).transpose(1, 0, 2)
     factors = jnp.pad(factors, ((0, 0), (0, 0), (0, width_keys - rows_g)))
     vmem = pl.BlockSpec(memory_space=pltpu.VMEM)
+    hbm = pl.BlockSpec(memory_space=pl.ANY)
     dma = pltpu.SemaphoreType.DMA
     flops = 4 * count * tokens * width * width_keys
     ortho, grad = pl.pallas_call(
@@ -460,9 +496,11 @@
             jax.ShapeDtypeStruct((count - 1, rows), F32),
             jax.ShapeDtypeStruct((1, rows), F32),
         ),
-        in_specs=[vmem] * 5,
+        in_specs=[hbm, hbm, hbm, vmem, hbm],
         out_specs=(vmem, vmem),
         scratch_shapes=[
+            pltpu.VMEM((tokens, width), jnp.bfloat16),
+            pltpu.VMEM((tokens, width_keys), jnp.bfloat16),
             pltpu.VMEM((n * 2 * groups, rows_g + PAD, width_keys), jnp.bfloat16),
             pltpu.VMEM((count * tokens, 2 * rows_g), jnp.bfloat16),
             pltpu.VMEM((count * tokens, width_keys), F32),
@@ -471,7 +509,9 @@
             pltpu.VMEM((n, count, rows), F32),
             pltpu.VMEM((n_dp, count, rows), F32),
             pltpu.VMEM((n, count - 1, 128), F32),
-            pltpu.VMEM((tokens, 128), F32),
+            pltpu.VMEM((tokens, width), F32),
+            dma((3, 2 * groups)),
+            dma((2,)),
             dma((9, steps)),
             dma((8, steps)),
             dma((n,)),
@@ -482,7 +522,7 @@
             dma((n,)),
         ],
         compiler_params=pltpu.CompilerParams(
-            collective_id=0, has_side_effects=True, vmem_limit_bytes=48 * 1024 * 1024
+            collective_id=0, has_side_effects=True, vmem_limit_bytes=56 * 1024 * 1024
         ),
         cost_estimate=pl.CostEstimate(flops=flops, bytes_accessed=4 * 2**20, transcendentals=0),
     )(activations, key_weight, factors, key_gain[None], cotangent)

time: 95.2 us -> 88.4 us (0.929)
  Pallas kernels: 87.1 us -> 82.6 us
  local copies, waits for them, and re-layouts: 6.36 us -> 4.04 us
    pallas_call x1, Pallas kernels: 87.1 us -> 82.6 us  [per_device(): pl.pallas_call(functools.partial(kernel, n, n_dp, groups, tokens * n * n_...]
    unnamed x10 -> x2, local copies, waits for them, and re-layouts: 5.58 us -> 2.65 us
where the time goes in v2:
time: 88.4 us; the launch traced here: 88.1 us
  Pallas kernels  82.6 us (93%)
  local copies, waits for them, and re-layouts  4.04 us (5%)
    pallas_call x1, Pallas kernels, per_device(): pl.pallas_call(functools.partial(kernel, n, n_dp, groups, tokens * n * n_...  82.6 us
    unnamed x2, local copies, waits for them, and re-layouts  2.65 us

profile of v2, /device:TPU:0, one launch (start us, length us, event | category | flops | bytes accessed | tf_op | source)
XLA Modules:
  0.0 88.1 jit_solution(17857091109690956299)
XLA Ops:
  0.6 0.1 pad.7.clone
  0.7 0.7 concatenate.11
  1.4 0.8 maximum_bitcast_fusion
  2.2 0.6 pad.4.dg_ref
  2.8 82.6 %shard_map.77 = (f32[8,1024]{1,0:T(8,128)}, f32[1,1024]{1,0:T(1,128)}) custom-call(bf16[128,8192]{1,0:T(8,128)(2,1)} %act_in.1, bf16[1024,512]{1,0:T(8,128)(2,1)} %w_ref.1, bf16[4,16,512]{2,1,0:T(8,128)(2,1)} %pad.4.dg_ref, f32[1,128]{1,0:T(1,128)} %bitcast.11, bf16[128,512]{1,0:T(8,128)(2,1)} %cot_in.1), custom_call_target="tpu_custom_call" | custom-call | flops 19327352832 | bytes 4194304 | tf_op jit(solution)/shard_map/pallas_call | solution.py:493
  85.5 1.4 %copy.11 = f32[1024,8]{0,1:T(8,128)} copy(f32[1024,8]{0,1:T(8,128)} %bitcast.8) | data formatting | bytes 65536
  86.8 1.3 %copy.12 = f32[1024]{0:T(1024)} copy(f32[1024]{0:T(1024)} %bitcast.10) | data formatting | bytes 8192
  (1 shorter events, 0.0 us)

commit v3 on v2

--- a/solution.py
+++ b/solution.py
@@ -168,7 +168,6 @@
 
         start(X, g, True)
 
-    acc[...] = jnp.zeros_like(acc)
     act_copy.wait()
 
     width = act_ref.shape[1]
@@ -186,7 +185,9 @@
 
     def normalize(q, _):
         cols = pl.ds(pl.multiple_of(q * 512, 512), 512)
-        nbuf[:, cols] = act_ref[:, cols].astype(F32) * rstd
+        normed = act_ref[:, cols].astype(F32) * rstd
+        nbuf[:, cols] = normed
+        act_ref[:, cols] = normed.astype(jnp.bfloat16)
         return 0
 
     lax.fori_loop(0, width // 512, normalize, 0)
@@ -199,29 +200,29 @@
             [wbuf[at, 0 : 2 * unit], wbuf[at, 2 * unit + PAD : 4 * unit + PAD]], axis=0
         )
 
-    def forward(zp, xp, g):
-        for cp in range(2):
-            at = place(zp, xp, cp, g)
-            normed = normed_at((zp * 2 + xp) * rows + (cp * groups + g) * rows_g, rows_g)
-            factors = wbuf[at, 2 * unit : 2 * unit + PAD, 0:rows_g].astype(F32)
-            for j in range(count):
-                lifted[j * tokens : (j + 1) * tokens, cp * rows_g : (cp + 1) * rows_g] = (
-                    normed * factors[j : j + 1]
-                ).astype(jnp.bfloat16)
-        weight = jnp.concatenate(
-            [weight_at(place(zp, xp, 0, g)), weight_at(place(zp, xp, 1, g))], axis=0
-        )
+    def forward(blocks, fresh=False):
+        weights = []
+        for b, (zp, xp, g) in enumerate(blocks):
+            for cp in range(2):
+                at = place(zp, xp, cp, g)
+                feature = (zp * 2 + xp) * rows + (cp * groups + g) * rows_g
+                normed = act_ref[:, pl.ds(pl.multiple_of(feature, 128), rows_g)]
+                factors = wbuf[at, 2 * unit : 2 * unit + PAD, 0:rows_g].astype(F32)
+                to = (2 * b + cp) * rows_g
+                for j in range(count):
+                    factor = jnp.broadcast_to(factors[j : j + 1], (16, rows_g))
+                    factor = jnp.concatenate([factor.astype(jnp.bfloat16)] * (tokens // 16), axis=0)
+                    lifted[j * tokens : (j + 1) * tokens, to : to + rows_g] = normed * factor
+                weights.append(weight_at(at))
+        weight = jnp.concatenate(weights, axis=0)
         for h in range(2):
             half = slice(h * 256, (h + 1) * 256)
-            acc[:, half] += jnp.dot(
-                lifted[...], weight[:, half], preferred_element_type=F32
+            product = jnp.dot(
+                lifted[:, 0 : len(weights) * rows_g], weight[:, half], preferred_element_type=F32
             )
-
-    def forward_own(g, _):
-        forward(z, x, g)
-        return 0
-
-    lax.fori_loop(0, groups, forward_own, 0)
+            acc[:, half] = product if fresh else acc[:, half] + product
+
+    forward([(z, x, g) for g in range(groups)], True)
 
     def cross_arrived(i, first):
         arrive(X, i, first)
@@ -275,7 +276,6 @@
             start(DY2, i2)
             arrive(DZ, i2)
             arrive(DY1, i2)
-            forward(source(i2 // groups)[0], x, lax.rem(i2, groups))
 
         i3 = t + groups - 3
 
@@ -289,9 +289,17 @@
             arrive(DX, i3)
             arrive(DY2, i3)
 
-        @pl.when((i3 >= 0) & (i3 < steps))
-        def _():
-            forward(source(i3 // groups)[0], 1 - x, lax.rem(i3, groups))
+        own = (source(i2 // groups)[0], x, lax.rem(i2, groups))
+        cross = (source(i3 // groups)[0], 1 - x, lax.rem(i3, groups))
+        both = (i2 >= groups) & (i2 < steps)
+
+        @pl.when(both)
+        def _():
+            forward([own, cross])
+
+        @pl.when((i3 >= 0) & (i3 < steps) & ((i2 < groups) | (i2 >= steps)))
+        def _():
+            forward([cross])
 
         return 0
 
@@ -502,7 +510,7 @@
             pltpu.VMEM((tokens, width), jnp.bfloat16),
             pltpu.VMEM((tokens, width_keys), jnp.bfloat16),
             pltpu.VMEM((n * 2 * groups, rows_g + PAD, width_keys), jnp.bfloat16),
-            pltpu.VMEM((count * tokens, 2 * rows_g), jnp.bfloat16),
+            pltpu.VMEM((count * tokens, 4 * rows_g), jnp.bfloat16),
             pltpu.VMEM((count * tokens, width_keys), F32),
             pltpu.VMEM((count * tokens, width_keys), jnp.bfloat16),
             pltpu.VMEM((n, count, rows), F32),

time: 88.4 us -> 88.6 us (level)
  no operation moved by 1% of the time
where the time goes in v3:
time: 88.6 us; the launch traced here: 88.3 us
  Pallas kernels  82.9 us (94%)
  local copies, waits for them, and re-layouts  4.04 us (5%)
    pallas_call x1, Pallas kernels, per_device(): pl.pallas_call(functools.partial(kernel, n, n_dp, groups, tokens * n * n_...  82.9 us
    unnamed x2, local copies, waits for them, and re-layouts  2.65 us

profile of v3, /device:TPU:0, one launch (start us, length us, event | category | flops | bytes accessed | tf_op | source)
XLA Modules:
  0.0 88.3 jit_solution(2418496068660846650)
XLA Ops:
  0.6 0.1 pad.7.clone
  0.7 0.7 concatenate.11
  1.4 0.8 maximum_bitcast_fusion
  2.2 0.6 pad.4.dg_ref
  2.8 82.9 %shard_map.77 = (f32[8,1024]{1,0:T(8,128)}, f32[1,1024]{1,0:T(1,128)}) custom-call(bf16[128,8192]{1,0:T(8,128)(2,1)} %act_in.1, bf16[1024,512]{1,0:T(8,128)(2,1)} %w_ref.1, bf16[4,16,512]{2,1,0:T(8,128)(2,1)} %pad.4.dg_ref, f32[1,128]{1,0:T(1,128)} %bitcast.11, bf16[128,512]{1,0:T(8,128)(2,1)} %cot_in.1), custom_call_target="tpu_custom_call" | custom-call | flops 19327352832 | bytes 4194304 | tf_op jit(solution)/shard_map/pallas_call | solution.py:501
  85.7 1.4 %copy.11 = f32[1024,8]{0,1:T(8,128)} copy(f32[1024,8]{0,1:T(8,128)} %bitcast.8) | data formatting | bytes 65536
  87.1 1.3 %copy.12 = f32[1024]{0:T(1024)} copy(f32[1024]{0:T(1024)} %bitcast.10) | data formatting | bytes 8192
  (1 shorter events, 0.0 us)

commit v4 on v3

--- a/solution.py
+++ b/solution.py
@@ -22,7 +22,7 @@
     n, n_dp, groups, total_tokens,
     act_in, w_ref, dg_ref, key_gain_ref, cot_in,
     ortho_ref, grad_ref,
-    act_ref, cot_ref, wbuf, lifted, acc, back, part, rbuf, xbuf, gbuf, nbuf, own_sem, in_sem,
+    act_ref, cot_ref, wbuf, turned, lifted, acc, back, part, rbuf, xbuf, gbuf, nbuf, own_sem, in_sem,
     send_sem, recv_sem, part_send, part_recv, dp_send, dp_recv, gram_send, gram_recv,
 ):
     line = n // 2
@@ -185,9 +185,7 @@
 
     def normalize(q, _):
         cols = pl.ds(pl.multiple_of(q * 512, 512), 512)
-        normed = act_ref[:, cols].astype(F32) * rstd
-        nbuf[:, cols] = normed
-        act_ref[:, cols] = normed.astype(jnp.bfloat16)
+        nbuf[:, cols] = act_ref[:, cols].astype(F32) * rstd
         return 0
 
     lax.fori_loop(0, width // 512, normalize, 0)
@@ -206,14 +204,15 @@
             for cp in range(2):
                 at = place(zp, xp, cp, g)
                 feature = (zp * 2 + xp) * rows + (cp * groups + g) * rows_g
-                normed = act_ref[:, pl.ds(pl.multiple_of(feature, 128), rows_g)]
+                normed = normed_at(feature, rows_g)
                 factors = wbuf[at, 2 * unit : 2 * unit + PAD, 0:rows_g].astype(F32)
                 to = (2 * b + cp) * rows_g
                 for j in range(count):
-                    factor = jnp.broadcast_to(factors[j : j + 1], (16, rows_g))
-                    factor = jnp.concatenate([factor.astype(jnp.bfloat16)] * (tokens // 16), axis=0)
-                    lifted[j * tokens : (j + 1) * tokens, to : to + rows_g] = normed * factor
+                    lifted[j * tokens : (j + 1) * tokens, to : to + rows_g] = (
+                        normed * factors[j : j + 1]
+                    ).astype(jnp.bfloat16)
                 weights.append(weight_at(at))
+                turned[:, pl.ds(pl.multiple_of(feature, 128), rows_g)] = weights[-1].T
         weight = jnp.concatenate(weights, axis=0)
         for h in range(2):
             half = slice(h * 256, (h + 1) * 256)
@@ -337,12 +336,10 @@
 
     def terms_of(owner):
         def one_pair(pair, _):
-            cg = owner * 2 * groups + 2 * pair
-            weight = jnp.concatenate([weight_at(cg), weight_at(cg + 1)], axis=0)
-            normed = normed_at(owner * rows + pair * 2 * rows_g, 2 * rows_g)
-            product = lax.dot_general(
-                back[...], weight, (((1,), (1,)), ((), ())), preferred_element_type=F32
-            )
+            feature = owner * rows + pair * 2 * rows_g
+            weight = turned[:, pl.ds(pl.multiple_of(feature, 128), 2 * rows_g)]
+            normed = normed_at(feature, 2 * rows_g)
+            product = jnp.dot(back[...], weight, preferred_element_type=F32)
             cols = pl.ds(pl.multiple_of(pair * 2 * rows_g, 128), 2 * rows_g)
             for j in range(count):
                 part[owner, j : j + 1, cols] = jnp.sum(
@@ -510,6 +507,7 @@
             pltpu.VMEM((tokens, width), jnp.bfloat16),
             pltpu.VMEM((tokens, width_keys), jnp.bfloat16),
             pltpu.VMEM((n * 2 * groups, rows_g + PAD, width_keys), jnp.bfloat16),
+            pltpu.VMEM((width_keys, width), jnp.bfloat16),
             pltpu.VMEM((count * tokens, 4 * rows_g), jnp.bfloat16),
             pltpu.VMEM((count * tokens, width_keys), F32),
             pltpu.VMEM((count * tokens, width_keys), jnp.bfloat16),

time: 88.6 us -> 88.5 us (level)
  no operation moved by 1% of the time
where the time goes in v4:
time: 88.5 us; the launch traced here: 88.1 us
  Pallas kernels  82.7 us (93%)
  local copies, waits for them, and re-layouts  4.04 us (5%)
    pallas_call x1, Pallas kernels, per_device(): pl.pallas_call(functools.partial(kernel, n, n_dp, groups, tokens * n * n_...  82.7 us
    unnamed x2, local copies, waits for them, and re-layouts  2.65 us

profile of v4, /device:TPU:0, one launch (start us, length us, event | category | flops | bytes accessed | tf_op | source)
XLA Modules:
  0.0 88.1 jit_solution(3721897019371866971)
XLA Ops:
  0.6 0.1 pad.7.clone
  0.7 0.7 concatenate.11
  1.4 0.8 maximum_bitcast_fusion
  2.2 0.6 pad.4.dg_ref
  2.8 82.7 %shard_map.77 = (f32[8,1024]{1,0:T(8,128)}, f32[1,1024]{1,0:T(1,128)}) custom-call(bf16[128,8192]{1,0:T(8,128)(2,1)} %act_in.1, bf16[1024,512]{1,0:T(8,128)(2,1)} %w_ref.1, bf16[4,16,512]{2,1,0:T(8,128)(2,1)} %pad.4.dg_ref, f32[1,128]{1,0:T(1,128)} %bitcast.11, bf16[128,512]{1,0:T(8,128)(2,1)} %cot_in.1), custom_call_target="tpu_custom_call" | custom-call | flops 19327352832 | bytes 4194304 | tf_op jit(solution)/shard_map/pallas_call | solution.py:498
  85.5 1.4 %copy.11 = f32[1024,8]{0,1:T(8,128)} copy(f32[1024,8]{0,1:T(8,128)} %bitcast.8) | data formatting | bytes 65536
  86.9 1.3 %copy.12 = f32[1024]{0:T(1024)} copy(f32[1024]{0:T(1024)} %bitcast.10) | data formatting | bytes 8192
  (1 shorter events, 0.0 us)
